TPU v7x, 32 devices: a whole 2x2x4 slice. The times are simulated.
32 devices in a mesh: orb: 4 (over y, x), dom: 8 (over z, core).
Axes of the slice: x: 2, y: 2, z: 4, core: 2. Of those that a mesh axis runs over, the one named last changes fastest.
Arguments:
- orbitals: float32 [8, 40, 32, 128], P('orb', 'dom'), may hold values from -8 to 8
- face_metric: float32 [3, 40, 32, 128], P(None, 'dom'), may hold values from 0.2 to 2.2
- cross_metric: float32 [3, 40, 32, 128], P(None, 'dom'), may hold values from -0.25 to 0.25
- screen: float32 [40, 32, 128], P('dom'), may hold values from 0.1 to 0.4
- turn_orbital: int32 [4], replicated, may hold values from 0 to 7, as said below
Outputs:
- exchange: float32 [8, 40, 32, 128], P('orb', 'dom')
Inputs may be any that keep to these rules, and one draw needn't show every extreme that they name: `turn_orbital`: orbital numbers; both 0 and 7 occur, and a number may recur.
All inputs are finite; a program needn't handle non-finite values.
Results may differ from a plain program's by a relative error of at most 0.0001.
Values sent between devices are 32-bit elements; how exact they have to be, the bound alone decides.
No kernel may reach another device: no remote copies, remote signals or barrier semaphores. Data moves between devices by JAX's collectives and lax.ppermute only.
A program may use at most 64 MiB of HBM per device.

v0:
```python
import jax
import jax.numpy as jnp
from jax import lax
from jax.sharding import PartitionSpec as P

SWEEPS = 6


def extended(cells, sides, width):
    for axis, dim in sides:
        count = lax.axis_size(axis)
        ends = count - 1
        head = lax.slice_in_dim(cells, 0, width, axis=dim)
        tail = lax.slice_in_dim(cells, cells.shape[dim] - width, cells.shape[dim], axis=dim)
        cells = jnp.concatenate(
            [
                lax.ppermute(tail, axis, [(i, (i + 1) % count) for i in range(ends)]),
                cells,
                lax.ppermute(head, axis, [((i + 1) % count, i) for i in range(ends)]),
            ],
            axis=dim,
        )
    return cells


def from_root(block, axis, holder):
    block = jnp.where(lax.axis_index(axis) == holder, block, jnp.zeros_like(block))
    return lax.psum(block, axis)


def shifted(padded, along_x, along_y, along_z):
    cells_x = padded.shape[1] - 2
    cells_y = padded.shape[2] - 2
    cells_z = padded.shape[3] - 2
    return padded[
        :,
        1 + along_x : 1 + along_x + cells_x,
        1 + along_y : 1 + along_y + cells_y,
        1 + along_z : 1 + along_z + cells_z,
    ]


def coupled(padded, face, cross):
    total = face[0] * (shifted(padded, 1, 0, 0) + shifted(padded, -1, 0, 0))
    total = total + face[1] * (shifted(padded, 0, 1, 0) + shifted(padded, 0, -1, 0))
    total = total + face[2] * (shifted(padded, 0, 0, 1) + shifted(padded, 0, 0, -1))
    total = total + 0.25 * cross[0] * (
        shifted(padded, 1, 1, 0)
        + shifted(padded, -1, -1, 0)
        - shifted(padded, 1, -1, 0)
        - shifted(padded, -1, 1, 0)
    )
    total = total + 0.25 * cross[1] * (
        shifted(padded, 1, 0, 1)
        + shifted(padded, -1, 0, -1)
        - shifted(padded, 1, 0, -1)
        - shifted(padded, -1, 0, 1)
    )
    total = total + 0.25 * cross[2] * (
        shifted(padded, 0, 1, 1)
        + shifted(padded, 0, -1, -1)
        - shifted(padded, 0, 1, -1)
        - shifted(padded, 0, -1, 1)
    )
    return total


def diagonal_sum(face, cross, screen):
    return (
        screen
        + 2.0 * (face[0] + face[1] + face[2])
        + (jnp.abs(cross[0]) + jnp.abs(cross[1]) + jnp.abs(cross[2]))
    )


def relax(density, inverse, face, cross):
    iterate = density * inverse
    for sweep_index in range(SWEEPS - 1):
        padded = extended(iterate, (("dom", 1),), 1)
        padded = jnp.pad(padded, ((0, 0), (0, 0), (1, 1), (1, 1)))
        iterate = (density + coupled(padded, face, cross)) * inverse
    return iterate


def body(orbitals, face_metric, cross_metric, screen, turn_orbital):
    local_count = orbitals.shape[0]
    own_numbers = lax.axis_index("orb") * local_count + jnp.arange(local_count, dtype=jnp.int32)
    inverse = 1.0 / diagonal_sum(face_metric, cross_metric, screen)
    result = jnp.zeros_like(orbitals)
    for turn_index in range(turn_orbital.shape[0]):
        which = turn_orbital[turn_index]
        picked = lax.dynamic_index_in_dim(orbitals, which % local_count, 0, keepdims=True)
        chosen_wide = from_root(picked, "orb", which // local_count)
        density = orbitals * chosen_wide
        potentials = relax(density, inverse, face_metric, cross_metric)
        result = result + potentials * chosen_wide
        partial_sum = jnp.sum(potentials * orbitals, axis=0)
        summed = lax.psum(partial_sum, "orb")
        result = result + jnp.where(
            (own_numbers == which)[:, None, None, None], summed[None], jnp.float32(0.0)
        )
    return result


def solution(mesh):
    in_specs = (
        P("orb", "dom", None, None),
        P(None, "dom", None, None),
        P(None, "dom", None, None),
        P("dom", None, None),
        P(),
    )
    out_specs = P("orb", "dom", None, None)
    return jax.shard_map(body, mesh=mesh, in_specs=in_specs, out_specs=out_specs, check_vma=False)
```

profile of v0, /device:TPU:0, one launch (start us, length us, event | category | flops | bytes accessed | tf_op | source)
XLA Modules:
  0.0 248.8 jit_solution(2325780373418820243)
XLA Ops:
  20.0 45.8 %all-reduce.27.cloned.1.call-done = (f32[5,32,128]{2,1,0:T(8,128)}, f32[5,32,128]{2,1,0:T(8,128)}, f32[5,32,128]{2,1,0:T(8,128)}, f32[5,32,128]{2,1,0:T(8,128)}) async-done(((f32[5,32,128]{2,1,0:T(8,128)}, f32[5,32,128]{2,1,0:T(8,128)}, f32[5,32,128]{2,1,0:T(8,128)}, f32[5,32,128]{2,1,0:T(8,128)}), (f32[5,32,128]{2,1,0:T(8,128)}, f32[5,32,128]{2,1,0:T(8,128)}, f32[5,32,128]{2,1,0:T(8,128)}, ...) | async-done | bytes 327696 | tf_op jit(solution)/shard_map/psum | solution.py:28
  69.5 4.7 %collective-permute-start.21 = (f32[2,1,32,128]{3,2,1,0:T(8,128)S(1)}, f32[2,1,32,128]{3,2,1,0:T(8,128)S(1)}, u32[]{:S(2)}, u32[]{:S(2)}) collective-permute-start(f32[2,1,32,128]{3,2,1,0:T(8,128)S(1)} %get-tuple-element.49), channel_id=1, source_target_pairs={{0,1},{1,2},{2,3},{3,4},{4,5},{5,6},{6,7},{8,9},{9,10},{10,11},{11... | collective-permute-start | bytes 98312 | tf_op jit(solution)/shard_map/ppermute | solution.py:17
  74.3 3.6 %collective-permute-start.1 = (f32[2,1,32,128]{3,2,1,0:T(8,128)S(1)}, f32[2,1,32,128]{3,2,1,0:T(8,128)S(1)}, u32[]{:S(2)}, u32[]{:S(2)}) collective-permute-start(f32[2,1,32,128]{3,2,1,0:T(8,128)S(1)} %get-tuple-element.69), channel_id=1, source_target_pairs={{0,1},{1,2},{2,3},{3,4},{4,5},{5,6},{6,7},{8,9},{9,10},{10,11},{11... | collective-permute-start | bytes 98312 | tf_op jit(solution)/shard_map/ppermute | solution.py:17
  79.3 3.0 %collective-permute-start.11 = (f32[2,1,32,128]{3,2,1,0:T(8,128)S(1)}, f32[2,1,32,128]{3,2,1,0:T(8,128)S(1)}, u32[]{:S(2)}, u32[]{:S(2)}) collective-permute-start(f32[2,1,32,128]{3,2,1,0:T(8,128)S(1)} %get-tuple-element.59), channel_id=1, source_target_pairs={{0,1},{1,2},{2,3},{3,4},{4,5},{5,6},{6,7},{8,9},{9,10},{10,11},{11... | collective-permute-start | bytes 98312 | tf_op jit(solution)/shard_map/ppermute | solution.py:17
  86.3 4.7 %collective-permute-start.3 = (f32[2,1,32,128]{3,2,1,0:T(8,128)S(1)}, f32[2,1,32,128]{3,2,1,0:T(8,128)S(1)}, u32[]{:S(2)}, u32[]{:S(2)}) collective-permute-start(f32[2,1,32,128]{3,2,1,0:T(8,128)S(1)} %get-tuple-element.67), channel_id=1, source_target_pairs={{0,1},{1,2},{2,3},{3,4},{4,5},{5,6},{6,7},{8,9},{9,10},{10,11},{11... | collective-permute-start | bytes 98312 | tf_op jit(solution)/shard_map/ppermute | solution.py:17
  93.1 3.9 %collective-permute-start.13 = (f32[2,1,32,128]{3,2,1,0:T(8,128)S(1)}, f32[2,1,32,128]{3,2,1,0:T(8,128)S(1)}, u32[]{:S(2)}, u32[]{:S(2)}) collective-permute-start(f32[2,1,32,128]{3,2,1,0:T(8,128)S(1)} %get-tuple-element.57), channel_id=1, source_target_pairs={{0,1},{1,2},{2,3},{3,4},{4,5},{5,6},{6,7},{8,9},{9,10},{10,11},{11... | collective-permute-start | bytes 98312 | tf_op jit(solution)/shard_map/ppermute | solution.py:17
  99.2 4.4 %collective-permute-start.23 = (f32[2,1,32,128]{3,2,1,0:T(8,128)S(1)}, f32[2,1,32,128]{3,2,1,0:T(8,128)S(1)}, u32[]{:S(2)}, u32[]{:S(2)}) collective-permute-start(f32[2,1,32,128]{3,2,1,0:T(8,128)S(1)} %get-tuple-element.47), channel_id=1, source_target_pairs={{0,1},{1,2},{2,3},{3,4},{4,5},{5,6},{6,7},{8,9},{9,10},{10,11},{11... | collective-permute-start | bytes 98312 | tf_op jit(solution)/shard_map/ppermute | solution.py:17
  105.7 4.3 %collective-permute-start.33 = (f32[2,1,32,128]{3,2,1,0:T(8,128)S(1)}, f32[2,1,32,128]{3,2,1,0:T(8,128)S(1)}, u32[]{:S(2)}, u32[]{:S(2)}) collective-permute-start(f32[2,1,32,128]{3,2,1,0:T(8,128)S(1)} %get-tuple-element.37), channel_id=1, source_target_pairs={{0,1},{1,2},{2,3},{3,4},{4,5},{5,6},{6,7},{8,9},{9,10},{10,11},{11... | collective-permute-start | bytes 98312 | tf_op jit(solution)/shard_map/ppermute | solution.py:17
  112.1 4.3 %collective-permute-start.5 = (f32[2,1,32,128]{3,2,1,0:T(8,128)S(1)}, f32[2,1,32,128]{3,2,1,0:T(8,128)S(1)}, u32[]{:S(2)}, u32[]{:S(2)}) collective-permute-start(f32[2,1,32,128]{3,2,1,0:T(8,128)S(1)} %get-tuple-element.65), channel_id=1, source_target_pairs={{0,1},{1,2},{2,3},{3,4},{4,5},{5,6},{6,7},{8,9},{9,10},{10,11},{11... | collective-permute-start | bytes 98312 | tf_op jit(solution)/shard_map/ppermute | solution.py:17
  118.5 4.3 %collective-permute-start.15 = (f32[2,1,32,128]{3,2,1,0:T(8,128)S(1)}, f32[2,1,32,128]{3,2,1,0:T(8,128)S(1)}, u32[]{:S(2)}, u32[]{:S(2)}) collective-permute-start(f32[2,1,32,128]{3,2,1,0:T(8,128)S(1)} %get-tuple-element.55), channel_id=1, source_target_pairs={{0,1},{1,2},{2,3},{3,4},{4,5},{5,6},{6,7},{8,9},{9,10},{10,11},{11... | collective-permute-start | bytes 98312 | tf_op jit(solution)/shard_map/ppermute | solution.py:17
  124.9 4.3 %collective-permute-start.25 = (f32[2,1,32,128]{3,2,1,0:T(8,128)S(1)}, f32[2,1,32,128]{3,2,1,0:T(8,128)S(1)}, u32[]{:S(2)}, u32[]{:S(2)}) collective-permute-start(f32[2,1,32,128]{3,2,1,0:T(8,128)S(1)} %get-tuple-element.45), channel_id=1, source_target_pairs={{0,1},{1,2},{2,3},{3,4},{4,5},{5,6},{6,7},{8,9},{9,10},{10,11},{11... | collective-permute-start | bytes 98312 | tf_op jit(solution)/shard_map/ppermute | solution.py:17
  131.3 4.3 %collective-permute-start.35 = (f32[2,1,32,128]{3,2,1,0:T(8,128)S(1)}, f32[2,1,32,128]{3,2,1,0:T(8,128)S(1)}, u32[]{:S(2)}, u32[]{:S(2)}) collective-permute-start(f32[2,1,32,128]{3,2,1,0:T(8,128)S(1)} %get-tuple-element.35), channel_id=1, source_target_pairs={{0,1},{1,2},{2,3},{3,4},{4,5},{5,6},{6,7},{8,9},{9,10},{10,11},{11... | collective-permute-start | bytes 98312 | tf_op jit(solution)/shard_map/ppermute | solution.py:17
  137.7 4.3 %collective-permute-start.7 = (f32[2,1,32,128]{3,2,1,0:T(8,128)S(1)}, f32[2,1,32,128]{3,2,1,0:T(8,128)S(1)}, u32[]{:S(2)}, u32[]{:S(2)}) collective-permute-start(f32[2,1,32,128]{3,2,1,0:T(8,128)S(1)} %get-tuple-element.63), channel_id=1, source_target_pairs={{0,1},{1,2},{2,3},{3,4},{4,5},{5,6},{6,7},{8,9},{9,10},{10,11},{11... | collective-permute-start | bytes 98312 | tf_op jit(solution)/shard_map/ppermute | solution.py:17
  144.1 4.3 %collective-permute-start.17 = (f32[2,1,32,128]{3,2,1,0:T(8,128)S(1)}, f32[2,1,32,128]{3,2,1,0:T(8,128)S(1)}, u32[]{:S(2)}, u32[]{:S(2)}) collective-permute-start(f32[2,1,32,128]{3,2,1,0:T(8,128)S(1)} %get-tuple-element.53), channel_id=1, source_target_pairs={{0,1},{1,2},{2,3},{3,4},{4,5},{5,6},{6,7},{8,9},{9,10},{10,11},{11... | collective-permute-start | bytes 98312 | tf_op jit(solution)/shard_map/ppermute | solution.py:17
  150.6 4.3 %collective-permute-start.27 = (f32[2,1,32,128]{3,2,1,0:T(8,128)S(1)}, f32[2,1,32,128]{3,2,1,0:T(8,128)S(1)}, u32[]{:S(2)}, u32[]{:S(2)}) collective-permute-start(f32[2,1,32,128]{3,2,1,0:T(8,128)S(1)} %get-tuple-element.43), channel_id=1, source_target_pairs={{0,1},{1,2},{2,3},{3,4},{4,5},{5,6},{6,7},{8,9},{9,10},{10,11},{11... | collective-permute-start | bytes 98312 | tf_op jit(solution)/shard_map/ppermute | solution.py:17
  157.0 4.5 %collective-permute-start.37 = (f32[2,1,32,128]{3,2,1,0:T(8,128)S(1)}, f32[2,1,32,128]{3,2,1,0:T(8,128)S(1)}, u32[]{:S(2)}, u32[]{:S(2)}) collective-permute-start(f32[2,1,32,128]{3,2,1,0:T(8,128)S(1)} %get-tuple-element.33), channel_id=1, source_target_pairs={{0,1},{1,2},{2,3},{3,4},{4,5},{5,6},{6,7},{8,9},{9,10},{10,11},{11... | collective-permute-start | bytes 98312 | tf_op jit(solution)/shard_map/ppermute | solution.py:17
  163.5 4.3 %collective-permute-start.9 = (f32[2,1,32,128]{3,2,1,0:T(8,128)S(1)}, f32[2,1,32,128]{3,2,1,0:T(8,128)S(1)}, u32[]{:S(2)}, u32[]{:S(2)}) collective-permute-start(f32[2,1,32,128]{3,2,1,0:T(8,128)S(1)} %get-tuple-element.61), channel_id=1, source_target_pairs={{0,1},{1,2},{2,3},{3,4},{4,5},{5,6},{6,7},{8,9},{9,10},{10,11},{11... | collective-permute-start | bytes 98312 | tf_op jit(solution)/shard_map/ppermute | solution.py:17
  169.9 4.3 %collective-permute-start.19 = (f32[2,1,32,128]{3,2,1,0:T(8,128)S(1)}, f32[2,1,32,128]{3,2,1,0:T(8,128)S(1)}, u32[]{:S(2)}, u32[]{:S(2)}) collective-permute-start(f32[2,1,32,128]{3,2,1,0:T(8,128)S(1)} %get-tuple-element.51), channel_id=1, source_target_pairs={{0,1},{1,2},{2,3},{3,4},{4,5},{5,6},{6,7},{8,9},{9,10},{10,11},{11... | collective-permute-start | bytes 98312 | tf_op jit(solution)/shard_map/ppermute | solution.py:17
  176.4 4.3 %collective-permute-start.29 = (f32[2,1,32,128]{3,2,1,0:T(8,128)S(1)}, f32[2,1,32,128]{3,2,1,0:T(8,128)S(1)}, u32[]{:S(2)}, u32[]{:S(2)}) collective-permute-start(f32[2,1,32,128]{3,2,1,0:T(8,128)S(1)} %get-tuple-element.41), channel_id=1, source_target_pairs={{0,1},{1,2},{2,3},{3,4},{4,5},{5,6},{6,7},{8,9},{9,10},{10,11},{11... | collective-permute-start | bytes 98312 | tf_op jit(solution)/shard_map/ppermute | solution.py:17
  182.8 4.3 %collective-permute-start.39 = (f32[2,1,32,128]{3,2,1,0:T(8,128)S(1)}, f32[2,1,32,128]{3,2,1,0:T(8,128)S(1)}, u32[]{:S(2)}, u32[]{:S(2)}) collective-permute-start(f32[2,1,32,128]{3,2,1,0:T(8,128)S(1)} %get-tuple-element.31), channel_id=1, source_target_pairs={{0,1},{1,2},{2,3},{3,4},{4,5},{5,6},{6,7},{8,9},{9,10},{10,11},{11... | collective-permute-start | bytes 98312 | tf_op jit(solution)/shard_map/ppermute | solution.py:17
  189.1 2.5 %collective-permute-done.38 = f32[2,1,32,128]{3,2,1,0:T(8,128)S(1)} collective-permute-done((f32[2,1,32,128]{3,2,1,0:T(8,128)S(1)}, f32[2,1,32,128]{3,2,1,0:T(8,128)S(1)}, u32[]{:S(2)}, u32[]{:S(2)}) %collective-permute-start.38) | collective-permute-done | bytes 32800 | tf_op jit(solution)/shard_map/ppermute | solution.py:19
  191.8 2.7 %multiply_reduce_fusion.3 = (f32[5,32,128]{2,1,0:T(8,128)}, f32[5,32,128]{2,1,0:T(8,128)}, f32[5,32,128]{2,1,0:T(8,128)}, f32[5,32,128]{2,1,0:T(8,128)}, f32[2,5...) fusion(f32[2,5,32,128]{3,2,1,0:T(8,128)S(1)} %copy-done, ...), kind=kLoop, calls=%fused_computation.591 | loop fusion | flops 4833280 | bytes 13451264 | tf_op jit(solution)/shard_map/reduce_sum | solution.py:97
  197.1 43.0 %all-reduce.25.cloned.1.call-done = (f32[5,32,128]{2,1,0:T(8,128)}, f32[5,32,128]{2,1,0:T(8,128)}, f32[5,32,128]{2,1,0:T(8,128)}, f32[5,32,128]{2,1,0:T(8,128)}) async-done(((f32[5,32,128]{2,1,0:T(8,128)}, f32[5,32,128]{2,1,0:T(8,128)}, f32[5,32,128]{2,1,0:T(8,128)}, f32[5,32,128]{2,1,0:T(8,128)}), (f32[5,32,128]{2,1,0:T(8,128)}, f32[5,32,128]{2,1,0:T(8,128)}, f32[5,32,128]{2,1,0:T(8,128)}, ...) | async-done | bytes 327696 | tf_op jit(solution)/shard_map/psum | solution.py:98
  240.2 1.8 select_add_fusion
  (145 shorter events, 48.0 us)
Async XLA Ops:
  6.5 59.3 %all-reduce.27.cloned.1.call-start = ((), (), s32[]{:S(2)}) async-start(), calls=%async_computation.1 | async-start | bytes 655360 | tf_op jit(solution)/shard_map/psum | solution.py:28
  18.9 221.3 %all-reduce.25.cloned.1.call-start = ((), (), s32[]{:S(2)}) async-start(), calls=%async_computation | async-start | bytes 655360 | tf_op jit(solution)/shard_map/psum | solution.py:98
  66.9 30.9 %collective-permute-start.31 = (f32[2,1,32,128]{3,2,1,0:T(8,128)S(1)}, f32[2,1,32,128]{3,2,1,0:T(8,128)S(1)}, u32[]{:S(2)}, u32[]{:S(2)}) collective-permute-start(f32[2,1,32,128]{3,2,1,0:T(8,128)S(1)} %get-tuple-element.39), channel_id=1, source_target_pairs={{0,1},{1,2},{2,3},{3,4},{4,5},{5,6},{6,7},{8,9},{9,10},{10,11},{11... | collective-permute-start | bytes 98312 | tf_op jit(solution)/shard_map/ppermute | solution.py:17
  68.2 30.9 %collective-permute-start.30 = (f32[2,1,32,128]{3,2,1,0:T(8,128)S(1)}, f32[2,1,32,128]{3,2,1,0:T(8,128)S(1)}, u32[]{:S(2)}, u32[]{:S(2)}) collective-permute-start(f32[2,1,32,128]{3,2,1,0:T(8,128)S(1)} %get-tuple-element.40), channel_id=1, source_target_pairs={{1,0},{2,1},{3,2},{4,3},{5,4},{6,5},{7,6},{9,8},{10,9},{11,10},{12... | collective-permute-start | bytes 98312 | tf_op jit(solution)/shard_map/ppermute | solution.py:19
  69.5 22.3 %collective-permute-start.21 = (f32[2,1,32,128]{3,2,1,0:T(8,128)S(1)}, f32[2,1,32,128]{3,2,1,0:T(8,128)S(1)}, u32[]{:S(2)}, u32[]{:S(2)}) collective-permute-start(f32[2,1,32,128]{3,2,1,0:T(8,128)S(1)} %get-tuple-element.49), channel_id=1, source_target_pairs={{0,1},{1,2},{2,3},{3,4},{4,5},{5,6},{6,7},{8,9},{9,10},{10,11},{11... | collective-permute-start | bytes 98312 | tf_op jit(solution)/shard_map/ppermute | solution.py:17
  86.3 18.1 %collective-permute-start.3 = (f32[2,1,32,128]{3,2,1,0:T(8,128)S(1)}, f32[2,1,32,128]{3,2,1,0:T(8,128)S(1)}, u32[]{:S(2)}, u32[]{:S(2)}) collective-permute-start(f32[2,1,32,128]{3,2,1,0:T(8,128)S(1)} %get-tuple-element.67), channel_id=1, source_target_pairs={{0,1},{1,2},{2,3},{3,4},{4,5},{5,6},{6,7},{8,9},{9,10},{10,11},{11... | collective-permute-start | bytes 98312 | tf_op jit(solution)/shard_map/ppermute | solution.py:17
  93.1 17.7 %collective-permute-start.13 = (f32[2,1,32,128]{3,2,1,0:T(8,128)S(1)}, f32[2,1,32,128]{3,2,1,0:T(8,128)S(1)}, u32[]{:S(2)}, u32[]{:S(2)}) collective-permute-start(f32[2,1,32,128]{3,2,1,0:T(8,128)S(1)} %get-tuple-element.57), channel_id=1, source_target_pairs={{0,1},{1,2},{2,3},{3,4},{4,5},{5,6},{6,7},{8,9},{9,10},{10,11},{11... | collective-permute-start | bytes 98312 | tf_op jit(solution)/shard_map/ppermute | solution.py:17
  97.9 14.3 %collective-permute-start.12 = (f32[2,1,32,128]{3,2,1,0:T(8,128)S(1)}, f32[2,1,32,128]{3,2,1,0:T(8,128)S(1)}, u32[]{:S(2)}, u32[]{:S(2)}) collective-permute-start(f32[2,1,32,128]{3,2,1,0:T(8,128)S(1)} %get-tuple-element.58), channel_id=1, source_target_pairs={{1,0},{2,1},{3,2},{4,3},{5,4},{6,5},{7,6},{9,8},{10,9},{11,10},{12... | collective-permute-start | bytes 98312 | tf_op jit(solution)/shard_map/ppermute | solution.py:19
  99.2 18.0 %collective-permute-start.23 = (f32[2,1,32,128]{3,2,1,0:T(8,128)S(1)}, f32[2,1,32,128]{3,2,1,0:T(8,128)S(1)}, u32[]{:S(2)}, u32[]{:S(2)}) collective-permute-start(f32[2,1,32,128]{3,2,1,0:T(8,128)S(1)} %get-tuple-element.47), channel_id=1, source_target_pairs={{0,1},{1,2},{2,3},{3,4},{4,5},{5,6},{6,7},{8,9},{9,10},{10,11},{11... | collective-permute-start | bytes 98312 | tf_op jit(solution)/shard_map/ppermute | solution.py:17
  105.7 17.9 %collective-permute-start.33 = (f32[2,1,32,128]{3,2,1,0:T(8,128)S(1)}, f32[2,1,32,128]{3,2,1,0:T(8,128)S(1)}, u32[]{:S(2)}, u32[]{:S(2)}) collective-permute-start(f32[2,1,32,128]{3,2,1,0:T(8,128)S(1)} %get-tuple-element.37), channel_id=1, source_target_pairs={{0,1},{1,2},{2,3},{3,4},{4,5},{5,6},{6,7},{8,9},{9,10},{10,11},{11... | collective-permute-start | bytes 98312 | tf_op jit(solution)/shard_map/ppermute | solution.py:17
  112.1 17.9 %collective-permute-start.5 = (f32[2,1,32,128]{3,2,1,0:T(8,128)S(1)}, f32[2,1,32,128]{3,2,1,0:T(8,128)S(1)}, u32[]{:S(2)}, u32[]{:S(2)}) collective-permute-start(f32[2,1,32,128]{3,2,1,0:T(8,128)S(1)} %get-tuple-element.65), channel_id=1, source_target_pairs={{0,1},{1,2},{2,3},{3,4},{4,5},{5,6},{6,7},{8,9},{9,10},{10,11},{11... | collective-permute-start | bytes 98312 | tf_op jit(solution)/shard_map/ppermute | solution.py:17
  118.5 17.9 %collective-permute-start.15 = (f32[2,1,32,128]{3,2,1,0:T(8,128)S(1)}, f32[2,1,32,128]{3,2,1,0:T(8,128)S(1)}, u32[]{:S(2)}, u32[]{:S(2)}) collective-permute-start(f32[2,1,32,128]{3,2,1,0:T(8,128)S(1)} %get-tuple-element.55), channel_id=1, source_target_pairs={{0,1},{1,2},{2,3},{3,4},{4,5},{5,6},{6,7},{8,9},{9,10},{10,11},{11... | collective-permute-start | bytes 98312 | tf_op jit(solution)/shard_map/ppermute | solution.py:17
  124.9 17.9 %collective-permute-start.25 = (f32[2,1,32,128]{3,2,1,0:T(8,128)S(1)}, f32[2,1,32,128]{3,2,1,0:T(8,128)S(1)}, u32[]{:S(2)}, u32[]{:S(2)}) collective-permute-start(f32[2,1,32,128]{3,2,1,0:T(8,128)S(1)} %get-tuple-element.45), channel_id=1, source_target_pairs={{0,1},{1,2},{2,3},{3,4},{4,5},{5,6},{6,7},{8,9},{9,10},{10,11},{11... | collective-permute-start | bytes 98312 | tf_op jit(solution)/shard_map/ppermute | solution.py:17
  131.3 17.9 %collective-permute-start.35 = (f32[2,1,32,128]{3,2,1,0:T(8,128)S(1)}, f32[2,1,32,128]{3,2,1,0:T(8,128)S(1)}, u32[]{:S(2)}, u32[]{:S(2)}) collective-permute-start(f32[2,1,32,128]{3,2,1,0:T(8,128)S(1)} %get-tuple-element.35), channel_id=1, source_target_pairs={{0,1},{1,2},{2,3},{3,4},{4,5},{5,6},{6,7},{8,9},{9,10},{10,11},{11... | collective-permute-start | bytes 98312 | tf_op jit(solution)/shard_map/ppermute | solution.py:17
  137.7 17.9 %collective-permute-start.7 = (f32[2,1,32,128]{3,2,1,0:T(8,128)S(1)}, f32[2,1,32,128]{3,2,1,0:T(8,128)S(1)}, u32[]{:S(2)}, u32[]{:S(2)}) collective-permute-start(f32[2,1,32,128]{3,2,1,0:T(8,128)S(1)} %get-tuple-element.63), channel_id=1, source_target_pairs={{0,1},{1,2},{2,3},{3,4},{4,5},{5,6},{6,7},{8,9},{9,10},{10,11},{11... | collective-permute-start | bytes 98312 | tf_op jit(solution)/shard_map/ppermute | solution.py:17
  144.1 18.1 %collective-permute-start.17 = (f32[2,1,32,128]{3,2,1,0:T(8,128)S(1)}, f32[2,1,32,128]{3,2,1,0:T(8,128)S(1)}, u32[]{:S(2)}, u32[]{:S(2)}) collective-permute-start(f32[2,1,32,128]{3,2,1,0:T(8,128)S(1)} %get-tuple-element.53), channel_id=1, source_target_pairs={{0,1},{1,2},{2,3},{3,4},{4,5},{5,6},{6,7},{8,9},{9,10},{10,11},{11... | collective-permute-start | bytes 98312 | tf_op jit(solution)/shard_map/ppermute | solution.py:17
  149.2 14.3 %collective-permute-start.16 = (f32[2,1,32,128]{3,2,1,0:T(8,128)S(1)}, f32[2,1,32,128]{3,2,1,0:T(8,128)S(1)}, u32[]{:S(2)}, u32[]{:S(2)}) collective-permute-start(f32[2,1,32,128]{3,2,1,0:T(8,128)S(1)} %get-tuple-element.54), channel_id=1, source_target_pairs={{1,0},{2,1},{3,2},{4,3},{5,4},{6,5},{7,6},{9,8},{10,9},{11,10},{12... | collective-permute-start | bytes 98312 | tf_op jit(solution)/shard_map/ppermute | solution.py:19
  150.6 18.1 %collective-permute-start.27 = (f32[2,1,32,128]{3,2,1,0:T(8,128)S(1)}, f32[2,1,32,128]{3,2,1,0:T(8,128)S(1)}, u32[]{:S(2)}, u32[]{:S(2)}) collective-permute-start(f32[2,1,32,128]{3,2,1,0:T(8,128)S(1)} %get-tuple-element.43), channel_id=1, source_target_pairs={{0,1},{1,2},{2,3},{3,4},{4,5},{5,6},{6,7},{8,9},{9,10},{10,11},{11... | collective-permute-start | bytes 98312 | tf_op jit(solution)/shard_map/ppermute | solution.py:17
  155.6 14.3 %collective-permute-start.26 = (f32[2,1,32,128]{3,2,1,0:T(8,128)S(1)}, f32[2,1,32,128]{3,2,1,0:T(8,128)S(1)}, u32[]{:S(2)}, u32[]{:S(2)}) collective-permute-start(f32[2,1,32,128]{3,2,1,0:T(8,128)S(1)} %get-tuple-element.44), channel_id=1, source_target_pairs={{1,0},{2,1},{3,2},{4,3},{5,4},{6,5},{7,6},{9,8},{10,9},{11,10},{12... | collective-permute-start | bytes 98312 | tf_op jit(solution)/shard_map/ppermute | solution.py:19
  157.0 18.1 %collective-permute-start.37 = (f32[2,1,32,128]{3,2,1,0:T(8,128)S(1)}, f32[2,1,32,128]{3,2,1,0:T(8,128)S(1)}, u32[]{:S(2)}, u32[]{:S(2)}) collective-permute-start(f32[2,1,32,128]{3,2,1,0:T(8,128)S(1)} %get-tuple-element.33), channel_id=1, source_target_pairs={{0,1},{1,2},{2,3},{3,4},{4,5},{5,6},{6,7},{8,9},{9,10},{10,11},{11... | collective-permute-start | bytes 98312 | tf_op jit(solution)/shard_map/ppermute | solution.py:17
  162.2 14.1 %collective-permute-start.36 = (f32[2,1,32,128]{3,2,1,0:T(8,128)S(1)}, f32[2,1,32,128]{3,2,1,0:T(8,128)S(1)}, u32[]{:S(2)}, u32[]{:S(2)}) collective-permute-start(f32[2,1,32,128]{3,2,1,0:T(8,128)S(1)} %get-tuple-element.34), channel_id=1, source_target_pairs={{1,0},{2,1},{3,2},{4,3},{5,4},{6,5},{7,6},{9,8},{10,9},{11,10},{12... | collective-permute-start | bytes 98312 | tf_op jit(solution)/shard_map/ppermute | solution.py:19
  163.5 17.9 %collective-permute-start.9 = (f32[2,1,32,128]{3,2,1,0:T(8,128)S(1)}, f32[2,1,32,128]{3,2,1,0:T(8,128)S(1)}, u32[]{:S(2)}, u32[]{:S(2)}) collective-permute-start(f32[2,1,32,128]{3,2,1,0:T(8,128)S(1)} %get-tuple-element.61), channel_id=1, source_target_pairs={{0,1},{1,2},{2,3},{3,4},{4,5},{5,6},{6,7},{8,9},{9,10},{10,11},{11... | collective-permute-start | bytes 98312 | tf_op jit(solution)/shard_map/ppermute | solution.py:17
  168.6 14.1 %collective-permute-start.8 = (f32[2,1,32,128]{3,2,1,0:T(8,128)S(1)}, f32[2,1,32,128]{3,2,1,0:T(8,128)S(1)}, u32[]{:S(2)}, u32[]{:S(2)}) collective-permute-start(f32[2,1,32,128]{3,2,1,0:T(8,128)S(1)} %get-tuple-element.62), channel_id=1, source_target_pairs={{1,0},{2,1},{3,2},{4,3},{5,4},{6,5},{7,6},{9,8},{10,9},{11,10},{12... | collective-permute-start | bytes 98312 | tf_op jit(solution)/shard_map/ppermute | solution.py:19
  169.9 17.3 %collective-permute-start.19 = (f32[2,1,32,128]{3,2,1,0:T(8,128)S(1)}, f32[2,1,32,128]{3,2,1,0:T(8,128)S(1)}, u32[]{:S(2)}, u32[]{:S(2)}) collective-permute-start(f32[2,1,32,128]{3,2,1,0:T(8,128)S(1)} %get-tuple-element.51), channel_id=1, source_target_pairs={{0,1},{1,2},{2,3},{3,4},{4,5},{5,6},{6,7},{8,9},{9,10},{10,11},{11... | collective-permute-start | bytes 98312 | tf_op jit(solution)/shard_map/ppermute | solution.py:17
  (27 other events, 214.5 us)
Sparse Core Ops, SparseCore 0:
  19.0 46.7 all-reduce.26
  194.7 45.4 all-reduce.24
where the time goes:
time: 250 us; the launch traced here: 249 us
  starting transfers between devices  107 us (43%)
  waiting for transfers between devices  92 us (37%)
  between operations  24.8 us (10%)
  other arithmetic  22.2 us (9%)
    ppermute x20, starting transfers between devices, extended(): lax.ppermute(tail, axis, [(i, (i + 1) % count) for i in range(ends)])  81.4 us
    psum x1, waiting for transfers between devices, from_root(): return lax.psum(block, axis)  45.8 us
    psum x1, waiting for transfers between devices, body(): summed = lax.psum(partial_sum, 'orb')  43 us
    ppermute x20, starting transfers between devices, extended(): lax.ppermute(head, axis, [((i + 1) % count, i) for i in range(ends)])  26 us
    mul x16, other arithmetic, relax(): iterate = (density + coupled(padded, face, cross)) * inverse  8.83 us
  transfers between devices with their start and end apart: 42, of which 4 were waited for; matrix products, arithmetic and copies ran while one was open for 6% of the time, Pallas kernels for 0%

commit v1 on v0

v1 whole, which is shorter than its diff:
```python
import functools

import jax
import jax.numpy as jnp
from jax import lax
from jax.experimental import pallas as pl
from jax.experimental.pallas import tpu as pltpu
from jax.sharding import PartitionSpec as P

SWEEPS = 6
DEEP = SWEEPS - 1
BATCH = 4
LANES = 128
TOP = 7
TALL = 32
LIMIT = 24 * 1024 * 1024


def padded_to_tile(rows):
    return -(-rows // 8) * 8


class Sizes:
    def __init__(self, groups, mine, planes, height, turns):
        self.groups, self.mine, self.planes, self.turns = groups, mine, planes, turns
        self.height = height
        self.orbs = groups * mine
        self.rows = height // groups
        self.window = self.rows + 2 * DEEP
        self.inner = self.window - 2
        self.span = planes + 2 * DEEP
        self.edge = DEEP - 1
        self.orb_rows = mine * planes * self.window
        self.orb_pack = padded_to_tile(self.orb_rows)
        self.metric_at = DEEP * self.window
        self.orb_at = self.metric_at + 6 * self.edge * self.inner
        self.side_pack = padded_to_tile(self.orb_at + self.orb_rows)


def pack_kernel(sz, orb_ref, face_ref, cross_ref, screen_ref, *refs):
    pieces = refs[: sz.groups]
    far_ref, near_ref, inv_ref, met_ref, orb_pad, met_pad = refs[sz.groups :]
    group = lax.axis_index("orb")
    odd = lax.rem(lax.axis_index("dom"), 2)
    zeros = jnp.zeros((8, LANES), jnp.float32)
    end = 8 + sz.height
    for p in range(sz.planes):
        for j in range(sz.mine):
            orb_pad[j, p, 0:8] = zeros
            orb_pad[j, p, end : end + 8] = zeros
            orb_pad[j, p, 8:end] = orb_ref[j, p]
        diag = screen_ref[p] + 2.0 * (face_ref[0, p] + face_ref[1, p] + face_ref[2, p])
        diag = diag + (jnp.abs(cross_ref[0, p]) + jnp.abs(cross_ref[1, p]) + jnp.abs(cross_ref[2, p]))
        met_pad[6, p, 8:end] = 1.0 / diag
        for c in range(3):
            met_pad[c, p, 8:end] = face_ref[c, p]
            met_pad[3 + c, p, 8:end] = 0.25 * cross_ref[c, p]
        for c in range(7):
            met_pad[c, p, 0:8] = zeros
            met_pad[c, p, end : end + 8] = zeros
    own = 8 + group * sz.rows - DEEP
    for s in range(sz.groups):
        first = 8 + jnp.bitwise_xor(group, s) * sz.rows - DEEP
        for j in range(sz.mine):
            for p in range(sz.planes):
                at = (j * sz.planes + p) * sz.window
                pieces[s][at : at + sz.window] = orb_pad[j, p, pl.ds(first, sz.window)]
    for ref, from_end in ((far_ref, odd), (near_ref, 1 - odd)):
        first_inv = from_end * (sz.planes - DEEP)
        first_met = from_end * (sz.planes - sz.edge)
        for p in range(DEEP):
            at = p * sz.window
            ref[at : at + sz.window] = met_pad[6, first_inv + p, pl.ds(own, sz.window)]
        for c in range(6):
            for p in range(sz.edge):
                at = sz.metric_at + (c * sz.edge + p) * sz.inner
                ref[at : at + sz.inner] = met_pad[c, first_met + p, pl.ds(own + 1, sz.inner)]
        for j in range(sz.mine):
            for p in range(DEEP):
                at = sz.orb_at + (j * DEEP + p) * sz.window
                ref[at : at + sz.window] = orb_pad[j, first_inv + p, pl.ds(own, sz.window)]
    for p in range(sz.planes):
        inv_ref[p, 0 : sz.window] = met_pad[6, p, pl.ds(own, sz.window)]
        for c in range(6):
            met_ref[c, p, 0 : sz.inner] = met_pad[c, p, pl.ds(own + 1, sz.inner)]


def list_pairs(sz, group, turn_ref, first_ref, second_ref, weight_ref, seen_ref, mult_ref):
    def slot_of(k):
        return jnp.bitwise_xor(k // sz.mine, group) * sz.mine + lax.rem(k, sz.mine)

    for i in range(sz.orbs):
        seen_ref[i] = 0
        mult_ref[i] = 0
    slots = [slot_of(turn_ref[t]) for t in range(sz.turns)]
    for k in slots:
        mult_ref[k] = mult_ref[k] + 1
    count = jnp.int32(0)
    for k in slots:
        fresh = 1 - seen_ref[k]
        times = mult_ref[k]

        def step(i, count, k=k, fresh=fresh, times=times):
            first_ref[count] = k
            second_ref[count] = i
            weight_ref[count] = times + mult_ref[i]
            return count + fresh * (1 - seen_ref[i])

        count = lax.fori_loop(0, sz.orbs, step, count)
        seen_ref[k] = 1
    for i in range(BATCH):
        first_ref[count + i] = 0
        second_ref[count + i] = 0
        weight_ref[count + i] = 0
    return count


def relax_kernel(sz, turn_ref, *refs):
    gathered = refs[: sz.groups]
    far_ref, near_ref, far_rest, near_rest, inv_ref, met_ref = refs[sz.groups : sz.groups + 6]
    outs = refs[sz.groups + 6 : 2 * sz.groups + 6]
    orbs, inv, coef, start, ping, pong, total, first_ref, second_ref, weight_ref, seen_ref, mult_ref = refs[
        2 * sz.groups + 6 :
    ]
    group = lax.axis_index("orb")
    odd = lax.rem(lax.axis_index("dom"), 2)
    n, win = sz.planes, sz.window
    below, above = 0, n + DEEP
    far_at = jnp.where(odd == 1, above, below)
    near_at = jnp.where(odd == 1, below, above)
    zeros = jnp.zeros((8, LANES), jnp.float32)

    count = list_pairs(sz, group, turn_ref, first_ref, second_ref, weight_ref, seen_ref, mult_ref)

    if TOP + win < 25:
        for p in range(sz.span):
            for r in range(0, TALL, 8):
                inv[p, r : r + 8] = zeros
                for i in range(sz.orbs):
                    orbs[i, p, r : r + 8] = zeros
                if r < 16:
                    for c in range(6):
                        coef[c, p, r : r + 8] = zeros
    for p in range(n):
        inv[DEEP + p, TOP : TOP + win] = inv_ref[p, 0:win]
        for c in range(6):
            coef[c, DEEP + p, 0 : sz.inner] = met_ref[c, p, 0 : sz.inner]
        for s in range(sz.groups):
            for j in range(sz.mine):
                at = (j * n + p) * win
                orbs[s * sz.mine + j, DEEP + p, TOP : TOP + win] = gathered[s][at : at + win]
    for ref, rest, at in ((far_ref, far_rest, far_at), (near_ref, near_rest, near_at)):
        for p in range(DEEP):
            inv[at + p, TOP : TOP + win] = ref[p * win : (p + 1) * win]
            for j in range(sz.mine):
                row = sz.orb_at + (j * DEEP + p) * win
                orbs[j, at + p, TOP : TOP + win] = ref[row : row + win]
            for i in range(sz.orbs - sz.mine):
                row = (i // sz.mine) * sz.orb_pack + ((i % sz.mine) * n + p) * win
                orbs[sz.mine + i, at + p, TOP : TOP + win] = rest[row : row + win]
        met_first = at + jnp.where(at == 0, 1, 0)
        for c in range(6):
            for p in range(sz.edge):
                row = sz.metric_at + (c * sz.edge + p) * sz.inner
                coef[c, met_first + p, 0 : sz.inner] = ref[row : row + sz.inner]

    lane = lax.broadcasted_iota(jnp.int32, (8, LANES), 1)

    def prepare(p, carry):
        for r in (0, 8):
            scale = inv[p, 8 + r : 16 + r]
            fx, fy, fz, xy, xz, yz = [coef[c, p, r : r + 8] * scale for c in range(6)]
            coef[0, p, r : r + 8] = fx
            coef[1, p, r : r + 8] = fy
            coef[2, p, r : r + 8] = xy
            for at, values, sign in ((3, fz, 1.0), (4, xz, -1.0), (5, yz, -1.0)):
                up = jnp.where(lane == 0, 0.0, pltpu.roll(values, 1, 1))
                down = jnp.where(lane == LANES - 1, 0.0, pltpu.roll(values, LANES - 1, 1))
                coef[at, p, r : r + 8] = up
                coef[at + 3, p, r : r + 8] = sign * down
        return carry

    lax.fori_loop(1, sz.span - 1, prepare, 0)

    for f in range(BATCH):
        for p in range(sz.span):
            for buf in (ping, pong):
                buf[f, p, 0:8] = zeros
                buf[f, p, TALL - 8 : TALL] = zeros
    for i in range(sz.orbs):
        for p in range(n):
            total[i, p] = zeros

    def sweep(source, number, row, planes, put):
        values = {}

        def fetch(f, p):
            up = source[f, p, row + 1 : row + 9]
            down = source[f, p, row - 1 : row + 7]
            return source[f, p, row : row + 8], up - down, up + down

        for f in range(BATCH):
            values[f, planes[0] - 1] = fetch(f, planes[0] - 1)
            values[f, planes[0]] = fetch(f, planes[0])
        for p in planes:
            cs = [coef[c, p, row - 8 : row] for c in range(9)]
            for f in range(BATCH):
                values[f, p + 1] = fetch(f, p + 1)
                before, diff_before, _ = values.pop((f, p - 1))
                here, diff, both = values[f, p]
                after, diff_after, _ = values[f, p + 1]
                slope = after - before
                up = cs[3] * here + cs[4] * slope + cs[5] * diff
                down = cs[6] * here + cs[7] * slope + cs[8] * diff
                new = start[f, p, row : row + 8] + cs[0] * (after + before)
                new = new + cs[1] * both + cs[2] * (diff_after - diff_before)
                new = new + (pltpu.roll(up, LANES - 1, 1) + pltpu.roll(down, 1, 1))
                put(f, p, new)

    def batch(index, carry):
        base = index * BATCH
        firsts = [first_ref[base + f] for f in range(BATCH)]
        seconds = [second_ref[base + f] for f in range(BATCH)]
        for p in range(sz.span):
            for r, size in ((TOP, 8), (TOP + 8, 8), (TOP + 16, 2)):
                scale = inv[p, r : r + size]
                for f in range(BATCH):
                    start[f, p, r : r + size] = (
                        orbs[firsts[f], p, r : r + size] * orbs[seconds[f], p, r : r + size] * scale
                    )
        source = start
        for number in range(1, DEEP):
            target = ping if number % 2 else pong
            planes = list(range(number, sz.span - number))
            for row in (8, 16):

                def put(f, p, new, row=row, target=target):
                    target[f, p, row : row + 8] = new

                sweep(source, number, row, planes, put)
            source = target
        row = TOP + DEEP
        weights = []
        for f in range(BATCH):
            w = weight_ref[base + f]
            weights.append(
                (w.astype(jnp.float32), jnp.where(firsts[f] == seconds[f], 0, w).astype(jnp.float32))
            )

        def put(f, p, new):
            a, b = firsts[f], seconds[f]
            q = p - DEEP
            total[a, q] = total[a, q] + (weights[f][0] * new) * orbs[b, p, row : row + 8]
            total[b, q] = total[b, q] + (weights[f][1] * new) * orbs[a, p, row : row + 8]

        sweep(source, DEEP, row, list(range(DEEP, sz.span - DEEP)), put)
        return carry

    lax.fori_loop(0, (count + BATCH - 1) // BATCH, batch, 0)

    for s in range(sz.groups):
        for j in range(sz.mine):
            for p in range(n):
                outs[s][j, p] = total[s * sz.mine + j, p, 0 : sz.rows]


def unpack_kernel(sz, *refs):
    blocks, out_ref = refs[: sz.groups], refs[sz.groups]
    group = lax.axis_index("orb")
    for s in range(sz.groups):
        first = jnp.bitwise_xor(group, s) * sz.rows
        if sz.rows % 8 == 0:
            first = pl.multiple_of(first, 8)
        for j in range(sz.mine):
            for p in range(sz.planes):
                out_ref[j, p, pl.ds(first, sz.rows)] = blocks[s][j, p]


def body(groups, slabs, orbitals, face_metric, cross_metric, screen, turn_orbital):
    mine, planes, height, lanes = orbitals.shape
    sz = Sizes(groups, mine, planes, height, turn_orbital.shape[0])
    f32 = jnp.float32
    vmem = pl.BlockSpec(memory_space=pltpu.VMEM)
    smem = pl.BlockSpec(memory_space=pltpu.SMEM)
    params = pltpu.CompilerParams(vmem_limit_bytes=LIMIT)

    packed = pl.pallas_call(
        functools.partial(pack_kernel, sz),
        out_shape=[jax.ShapeDtypeStruct((sz.orb_pack, lanes), f32)] * groups
        + [jax.ShapeDtypeStruct((sz.side_pack, lanes), f32)] * 2
        + [
            jax.ShapeDtypeStruct((planes, 24, lanes), f32),
            jax.ShapeDtypeStruct((6, planes, 16, lanes), f32),
        ],
        in_specs=[vmem] * 4,
        out_specs=[vmem] * (groups + 4),
        scratch_shapes=[
            pltpu.VMEM((mine, planes, height + 16, lanes), f32),
            pltpu.VMEM((7, planes, height + 16, lanes), f32),
        ],
        compiler_params=params,
        name="pack",
    )(orbitals, face_metric, cross_metric, screen)
    pieces = packed[:groups]
    far, near, inverse, metric = packed[groups:]

    def swap(x, s):
        return lax.ppermute(x, "orb", [(i, i ^ s) for i in range(groups)])

    to_near = [(i, i ^ 1) for i in range(slabs)]
    to_far = [(i, ((i + 1) ^ 1) - 1) for i in range(1, slabs - 1)]
    gathered = [pieces[0]] + [swap(pieces[s], s) for s in range(1, groups)]
    far_side = lax.ppermute(far, "dom", to_far)
    near_side = lax.ppermute(near, "dom", to_near)
    rest = jnp.concatenate(gathered[1:], axis=0)
    far_rest = lax.ppermute(rest, "dom", to_far)
    near_rest = lax.ppermute(rest, "dom", to_near)

    room = sz.turns * sz.orbs + BATCH
    field = pltpu.VMEM((BATCH, sz.span, TALL, lanes), f32)
    shares = pl.pallas_call(
        functools.partial(relax_kernel, sz),
        out_shape=[jax.ShapeDtypeStruct((mine, planes, sz.rows, lanes), f32)] * groups,
        in_specs=[smem] + [vmem] * (groups + 6),
        out_specs=[vmem] * groups,
        scratch_shapes=[
            pltpu.VMEM((sz.orbs, sz.span, TALL, lanes), f32),
            pltpu.VMEM((sz.span, TALL, lanes), f32),
            pltpu.VMEM((9, sz.span, 16, lanes), f32),
            field,
            field,
            field,
            pltpu.VMEM((sz.orbs, planes, 8, lanes), f32),
            pltpu.SMEM((room,), jnp.int32),
            pltpu.SMEM((room,), jnp.int32),
            pltpu.SMEM((room,), jnp.int32),
            pltpu.SMEM((sz.orbs,), jnp.int32),
            pltpu.SMEM((sz.orbs,), jnp.int32),
        ],
        compiler_params=params,
        name="relax",
    )(turn_orbital, *gathered, far_side, near_side, far_rest, near_rest, inverse, metric)
    blocks = [shares[0]] + [swap(shares[s], s) for s in range(1, groups)]
    return pl.pallas_call(
        functools.partial(unpack_kernel, sz),
        out_shape=jax.ShapeDtypeStruct((mine, planes, height, lanes), f32),
        in_specs=[vmem] * groups,
        out_specs=vmem,
        compiler_params=params,
        name="unpack",
    )(*blocks)


def solution(mesh):
    in_specs = (
        P("orb", "dom", None, None),
        P(None, "dom", None, None),
        P(None, "dom", None, None),
        P("dom", None, None),
        P(),
    )
    out_specs = P("orb", "dom", None, None)
    return jax.shard_map(
        functools.partial(body, mesh.shape["orb"], mesh.shape["dom"]),
        mesh=mesh,
        in_specs=in_specs,
        out_specs=out_specs,
        check_vma=False,
    )
```

time: 250 us -> 41.3 us (0.17)
  the two profiles are of different devices: /device:TPU:0 before, /device:TPU:8 now
where the time goes in v1:
time: 41.3 us; the launch traced here: 41 us
  starting transfers between devices  14.4 us (35%)
  Pallas kernels  13.5 us (33%)
  waiting for transfers between devices  8.69 us (21%)
  local copies, waits for them, and re-layouts  4.37 us (11%)
    pallas_call x1, Pallas kernels, body(): pl.pallas_call(functools.partial(relax_kernel, sz), out_shape=[jax.ShapeD...  12.6 us
    ppermute x6, starting transfers between devices, swap(): return lax.ppermute(x, 'orb', [(i, i ^ s) for i in range(groups)])  7.11 us
    ppermute x6, waiting for transfers between devices, swap(): return lax.ppermute(x, 'orb', [(i, i ^ s) for i in range(groups)])  4.45 us
    unnamed x12, local copies, waits for them, and re-layouts  4.36 us
    ppermute x1, waiting for transfers between devices, body(): far_rest = lax.ppermute(rest, 'dom', to_far)  4.23 us
    ppermute x1, starting transfers between devices, body(): far_rest = lax.ppermute(rest, 'dom', to_far)  1.92 us
    ppermute x1, starting transfers between devices, body(): far_side = lax.ppermute(far, 'dom', to_far)  1.91 us
    ppermute x1, starting transfers between devices, body(): near_side = lax.ppermute(near, 'dom', to_near)  1.74 us
  transfers between devices with their start and end apart: 10, of which 5 were waited for; matrix products, arithmetic and copies ran while one was open for 0% of the time, Pallas kernels for 0%

profile of v1, /device:TPU:8, one launch (start us, length us, event | category | flops | bytes accessed | tf_op | source)
XLA Modules:
  0.0 41.0 jit_solution(17606971853805372429)
XLA Ops:
  0.0 0.9 %copy-done = f32[3,5,32,128]{3,2,1,0:T(8,128)S(1)} copy-done((f32[3,5,32,128]{3,2,1,0:T(8,128)S(1)}, f32[3,5,32,128]{3,2,1,0:T(8,128)}, u32[]{:S(2)}) %copy-start) | copy-done | bytes 245784
  0.9 0.9 %copy-done.1 = f32[3,5,32,128]{3,2,1,0:T(8,128)S(1)} copy-done((f32[3,5,32,128]{3,2,1,0:T(8,128)S(1)}, f32[3,5,32,128]{3,2,1,0:T(8,128)}, u32[]{:S(2)}) %copy-start.1) | copy-done | bytes 245784
  1.9 0.9 %copy-done.2 = f32[2,5,32,128]{3,2,1,0:T(8,128)S(1)} copy-done((f32[2,5,32,128]{3,2,1,0:T(8,128)S(1)}, f32[2,5,32,128]{3,2,1,0:T(8,128)}, u32[]{:S(2)}) %copy-start.2) | copy-done | bytes 163864
  2.8 0.9 %copy-done.3 = f32[5,32,128]{2,1,0:T(8,128)S(1)} copy-done((f32[5,32,128]{2,1,0:T(8,128)S(1)}, f32[5,32,128]{2,1,0:T(8,128)}, u32[]{:S(2)}) %copy-start.3) | copy-done | bytes 81944
  3.7 0.2 pack.1
  3.9 1.6 %collective-permute-start = (f32[184,128]{1,0:T(8,128)S(1)}, f32[184,128]{1,0:T(8,128)S(1)}, u32[]{:S(2)}, u32[]{:S(2)}) collective-permute-start(f32[184,128]{1,0:T(8,128)S(1)} %get-tuple-element.18), channel_id=1, source_target_pairs={{0,8},{8,0},{16,24},{24,16},{1,9},{9,1},{17,25},{25,17},{2,10},{10... | collective-permute-start | bytes 282632 | tf_op jit(solution)/shard_map/ppermute | solution.py:308
  5.4 1.5 %collective-permute-start.1 = (f32[184,128]{1,0:T(8,128)S(1)}, f32[184,128]{1,0:T(8,128)S(1)}, u32[]{:S(2)}, u32[]{:S(2)}) collective-permute-start(f32[184,128]{1,0:T(8,128)S(1)} %get-tuple-element.19), channel_id=1, source_target_pairs={{0,16},{8,24},{16,0},{24,8},{1,17},{9,25},{17,1},{25,9},{2,18},{10... | collective-permute-start | bytes 282632 | tf_op jit(solution)/shard_map/ppermute | solution.py:308
  6.9 0.5 %collective-permute-start.2 = (f32[184,128]{1,0:T(8,128)S(1)}, f32[184,128]{1,0:T(8,128)S(1)}, u32[]{:S(2)}, u32[]{:S(2)}) collective-permute-start(f32[184,128]{1,0:T(8,128)S(1)} %get-tuple-element.20), channel_id=1, source_target_pairs={{0,24},{8,16},{16,8},{24,0},{1,25},{9,17},{17,9},{25,1},{2,26},{10... | collective-permute-start | bytes 282632 | tf_op jit(solution)/shard_map/ppermute | solution.py:308
  7.4 1.9 %collective-permute-start.3 = (f32[656,128]{1,0:T(8,128)S(1)}, f32[656,128]{1,0:T(8,128)S(1)}, u32[]{:S(2)}, u32[]{:S(2)}) collective-permute-start(f32[656,128]{1,0:T(8,128)S(1)} %get-tuple-element.21), channel_id=1, source_target_pairs={{1,2},{2,1},{3,4},{4,3},{5,6},{6,5},{9,10},{10,9},{11,12},{12,11},... | collective-permute-start | bytes 1007624 | tf_op jit(solution)/shard_map/ppermute | solution.py:313
  9.3 1.7 %collective-permute-start.4 = (f32[656,128]{1,0:T(8,128)S(1)}, f32[656,128]{1,0:T(8,128)S(1)}, u32[]{:S(2)}, u32[]{:S(2)}) collective-permute-start(f32[656,128]{1,0:T(8,128)S(1)} %get-tuple-element.22), channel_id=1, source_target_pairs={{0,1},{1,0},{2,3},{3,2},{4,5},{5,4},{6,7},{7,6},{8,9},{9,8},{10,11... | collective-permute-start | bytes 1007624 | tf_op jit(solution)/shard_map/ppermute | solution.py:314
  11.1 0.0 collective-permute-done.1.refs_2_
  11.1 1.3 %collective-permute-done.2.refs_3_ = f32[184,128]{1,0:T(8,128)S(1)} collective-permute-done((f32[184,128]{1,0:T(8,128)S(1)}, f32[184,128]{1,0:T(8,128)S(1)}, u32[]{:S(2)}, u32[]{:S(2)}) %collective-permute-start.2) | collective-permute-done | bytes 94240 | tf_op jit(solution)/shard_map/ppermute | solution.py:308
  12.4 1.9 %collective-permute-start.5 = (f32[552,128]{1,0:T(8,128)S(1)}, f32[552,128]{1,0:T(8,128)S(1)}, u32[]{:S(2)}, u32[]{:S(2)}) collective-permute-start(f32[552,128]{1,0:T(8,128)S(1)} %constant_dynamic-update-slice_fusion), channel_id=1, source_target_pairs={{1,2},{2,1},{3,4},{4,3},{5,6},{6,5},{9,10},{10,9},{11,12},{12,11},... | collective-permute-start | bytes 847880 | tf_op jit(solution)/shard_map/ppermute | solution.py:316
  14.4 1.7 %collective-permute-start.6 = (f32[552,128]{1,0:T(8,128)S(1)}, f32[552,128]{1,0:T(8,128)S(1)}, u32[]{:S(2)}, u32[]{:S(2)}) collective-permute-start(f32[552,128]{1,0:T(8,128)S(1)} %constant_dynamic-update-slice_fusion), channel_id=1, source_target_pairs={{0,1},{1,0},{2,3},{3,2},{4,5},{5,4},{6,7},{7,6},{8,9},{9,8},{10,11... | collective-permute-start | bytes 847880 | tf_op jit(solution)/shard_map/ppermute | solution.py:317
  16.1 4.2 %collective-permute-done.5.refs_6_ = f32[552,128]{1,0:T(8,128)S(1)} collective-permute-done((f32[552,128]{1,0:T(8,128)S(1)}, f32[552,128]{1,0:T(8,128)S(1)}, u32[]{:S(2)}, u32[]{:S(2)}) %collective-permute-start.5) | collective-permute-done | bytes 282656 | tf_op jit(solution)/shard_map/ppermute | solution.py:316
  20.3 0.7 %copy-done.4 = s32[4]{0:T(128)S(1)} copy-done((s32[4]{0:T(128)S(1)}, s32[4]{0:T(128)}, u32[]{:S(2)}) %copy-start.4) | copy-done | bytes 40
  21.0 12.6 %relax.1 = (f32[2,5,8,128]{3,2,1,0:T(8,128)S(1)}, f32[2,5,8,128]{3,2,1,0:T(8,128)S(1)}, f32[2,5,8,128]{3,2,1,0:T(8,128)S(1)}, f32[2,5,8,128]{3,2,1,0:T(8,128)S(1)}) custom-call(s32[4]{0:T(128)S(1)} %copy-done.4, f32[184,128]{1,0:T(8,128)S(1)} %get-tuple-element.17.refs_0_, f32[184,128]{1,0:T(8,128)S(1)} %collective-permute-done.refs_1_, ...), custom_call_target="tpu_custom_call" | custom-call | tf_op jit(solution)/shard_map/relax/pallas_call | solution.py:321
  33.7 0.6 %collective-permute-start.7 = (f32[2,5,8,128]{3,2,1,0:T(8,128)S(1)}, f32[2,5,8,128]{3,2,1,0:T(8,128)S(1)}, u32[]{:S(2)}, u32[]{:S(2)}) collective-permute-start(f32[2,5,8,128]{3,2,1,0:T(8,128)S(1)} %get-tuple-element.26), channel_id=1, source_target_pairs={{0,8},{8,0},{16,24},{24,16},{1,9},{9,1},{17,25},{25,17},{2,10},{10... | collective-permute-start | bytes 122888 | tf_op jit(solution)/shard_map/ppermute | solution.py:308
  34.3 1.2 %collective-permute-start.8 = (f32[2,5,8,128]{3,2,1,0:T(8,128)S(1)}, f32[2,5,8,128]{3,2,1,0:T(8,128)S(1)}, u32[]{:S(2)}, u32[]{:S(2)}) collective-permute-start(f32[2,5,8,128]{3,2,1,0:T(8,128)S(1)} %get-tuple-element.27), channel_id=1, source_target_pairs={{0,16},{8,24},{16,0},{24,8},{1,17},{9,25},{17,1},{25,9},{2,18},{10... | collective-permute-start | bytes 122888 | tf_op jit(solution)/shard_map/ppermute | solution.py:308
  35.5 1.7 %collective-permute-start.9 = (f32[2,5,8,128]{3,2,1,0:T(8,128)S(1)}, f32[2,5,8,128]{3,2,1,0:T(8,128)S(1)}, u32[]{:S(2)}, u32[]{:S(2)}) collective-permute-start(f32[2,5,8,128]{3,2,1,0:T(8,128)S(1)} %get-tuple-element.28), channel_id=1, source_target_pairs={{0,24},{8,16},{16,8},{24,0},{1,25},{9,17},{17,9},{25,1},{2,26},{10... | collective-permute-start | bytes 122888 | tf_op jit(solution)/shard_map/ppermute | solution.py:308
  37.2 0.5 %collective-permute-done.7.refs_1_ = f32[2,5,8,128]{3,2,1,0:T(8,128)S(1)} collective-permute-done((f32[2,5,8,128]{3,2,1,0:T(8,128)S(1)}, f32[2,5,8,128]{3,2,1,0:T(8,128)S(1)}, u32[]{:S(2)}, u32[]{:S(2)}) %collective-permute-start.7) | collective-permute-done | bytes 40992 | tf_op jit(solution)/shard_map/ppermute | solution.py:308
  37.7 0.6 %collective-permute-done.8.refs_2_ = f32[2,5,8,128]{3,2,1,0:T(8,128)S(1)} collective-permute-done((f32[2,5,8,128]{3,2,1,0:T(8,128)S(1)}, f32[2,5,8,128]{3,2,1,0:T(8,128)S(1)}, u32[]{:S(2)}, u32[]{:S(2)}) %collective-permute-start.8) | collective-permute-done | bytes 40992 | tf_op jit(solution)/shard_map/ppermute | solution.py:308
  38.3 2.1 %collective-permute-done.9.refs_3_ = f32[2,5,8,128]{3,2,1,0:T(8,128)S(1)} collective-permute-done((f32[2,5,8,128]{3,2,1,0:T(8,128)S(1)}, f32[2,5,8,128]{3,2,1,0:T(8,128)S(1)}, u32[]{:S(2)}, u32[]{:S(2)}) %collective-permute-start.9) | collective-permute-done | bytes 40992 | tf_op jit(solution)/shard_map/ppermute | solution.py:308
  40.4 0.7 %unpack.1 = f32[2,5,32,128]{3,2,1,0:T(8,128)} custom-call(f32[2,5,8,128]{3,2,1,0:T(8,128)S(1)} %get-tuple-element.25.refs_0_, f32[2,5,8,128]{3,2,1,0:T(8,128)S(1)} %collective-permute-done.7.refs_1_, f32[2,5,8,128]{3,2,1,0:T(8,128)S(1)} %collective-permute-done.8.refs_2_, f32[2,5,8,128]{3,2,1,0:T(8,128)S(1)} %collective-permute-done.9.refs_3_), custom_call_target="tpu_custom_call" | custom-call | tf_op jit(solution)/shard_map/unpack/pallas_call | solution.py:344
  (12 shorter events, 0.0 us)
Async XLA Ops:
  0.0 0.9 %copy-start = (f32[3,5,32,128]{3,2,1,0:T(8,128)S(1)}, f32[3,5,32,128]{3,2,1,0:T(8,128)}, u32[]{:S(2)}) copy-start(f32[3,5,32,128]{3,2,1,0:T(8,128)} %face_ref.1) | copy-start | bytes 737284
  0.9 0.9 %copy-start.1 = (f32[3,5,32,128]{3,2,1,0:T(8,128)S(1)}, f32[3,5,32,128]{3,2,1,0:T(8,128)}, u32[]{:S(2)}) copy-start(f32[3,5,32,128]{3,2,1,0:T(8,128)} %cross_ref.1) | copy-start | bytes 737284
  1.9 0.9 %copy-start.2 = (f32[2,5,32,128]{3,2,1,0:T(8,128)S(1)}, f32[2,5,32,128]{3,2,1,0:T(8,128)}, u32[]{:S(2)}) copy-start(f32[2,5,32,128]{3,2,1,0:T(8,128)} %orb_ref.1) | copy-start | bytes 491524
  2.8 0.9 %copy-start.3 = (f32[5,32,128]{2,1,0:T(8,128)S(1)}, f32[5,32,128]{2,1,0:T(8,128)}, u32[]{:S(2)}) copy-start(f32[5,32,128]{2,1,0:T(8,128)} %screen_ref.1) | copy-start | bytes 245764
  3.9 7.2 %collective-permute-start = (f32[184,128]{1,0:T(8,128)S(1)}, f32[184,128]{1,0:T(8,128)S(1)}, u32[]{:S(2)}, u32[]{:S(2)}) collective-permute-start(f32[184,128]{1,0:T(8,128)S(1)} %get-tuple-element.18), channel_id=1, source_target_pairs={{0,8},{8,0},{16,24},{24,16},{1,9},{9,1},{17,25},{25,17},{2,10},{10... | collective-permute-start | bytes 282632 | tf_op jit(solution)/shard_map/ppermute | solution.py:308
  5.4 5.7 %collective-permute-start.1 = (f32[184,128]{1,0:T(8,128)S(1)}, f32[184,128]{1,0:T(8,128)S(1)}, u32[]{:S(2)}, u32[]{:S(2)}) collective-permute-start(f32[184,128]{1,0:T(8,128)S(1)} %get-tuple-element.19), channel_id=1, source_target_pairs={{0,16},{8,24},{16,0},{24,8},{1,17},{9,25},{17,1},{25,9},{2,18},{10... | collective-permute-start | bytes 282632 | tf_op jit(solution)/shard_map/ppermute | solution.py:308
  6.9 5.5 %collective-permute-start.2 = (f32[184,128]{1,0:T(8,128)S(1)}, f32[184,128]{1,0:T(8,128)S(1)}, u32[]{:S(2)}, u32[]{:S(2)}) collective-permute-start(f32[184,128]{1,0:T(8,128)S(1)} %get-tuple-element.20), channel_id=1, source_target_pairs={{0,24},{8,16},{16,8},{24,0},{1,25},{9,17},{17,9},{25,1},{2,26},{10... | collective-permute-start | bytes 282632 | tf_op jit(solution)/shard_map/ppermute | solution.py:308
  7.4 8.7 %collective-permute-start.3 = (f32[656,128]{1,0:T(8,128)S(1)}, f32[656,128]{1,0:T(8,128)S(1)}, u32[]{:S(2)}, u32[]{:S(2)}) collective-permute-start(f32[656,128]{1,0:T(8,128)S(1)} %get-tuple-element.21), channel_id=1, source_target_pairs={{1,2},{2,1},{3,4},{4,3},{5,6},{6,5},{9,10},{10,9},{11,12},{12,11},... | collective-permute-start | bytes 1007624 | tf_op jit(solution)/shard_map/ppermute | solution.py:313
  9.3 6.8 %collective-permute-start.4 = (f32[656,128]{1,0:T(8,128)S(1)}, f32[656,128]{1,0:T(8,128)S(1)}, u32[]{:S(2)}, u32[]{:S(2)}) collective-permute-start(f32[656,128]{1,0:T(8,128)S(1)} %get-tuple-element.22), channel_id=1, source_target_pairs={{0,1},{1,0},{2,3},{3,2},{4,5},{5,4},{6,7},{7,6},{8,9},{9,8},{10,11... | collective-permute-start | bytes 1007624 | tf_op jit(solution)/shard_map/ppermute | solution.py:314
  12.4 7.9 %collective-permute-start.5 = (f32[552,128]{1,0:T(8,128)S(1)}, f32[552,128]{1,0:T(8,128)S(1)}, u32[]{:S(2)}, u32[]{:S(2)}) collective-permute-start(f32[552,128]{1,0:T(8,128)S(1)} %constant_dynamic-update-slice_fusion), channel_id=1, source_target_pairs={{1,2},{2,1},{3,4},{4,3},{5,6},{6,5},{9,10},{10,9},{11,12},{12,11},... | collective-permute-start | bytes 847880 | tf_op jit(solution)/shard_map/ppermute | solution.py:316
  14.4 6.0 %collective-permute-start.6 = (f32[552,128]{1,0:T(8,128)S(1)}, f32[552,128]{1,0:T(8,128)S(1)}, u32[]{:S(2)}, u32[]{:S(2)}) collective-permute-start(f32[552,128]{1,0:T(8,128)S(1)} %constant_dynamic-update-slice_fusion), channel_id=1, source_target_pairs={{0,1},{1,0},{2,3},{3,2},{4,5},{5,4},{6,7},{7,6},{8,9},{9,8},{10,11... | collective-permute-start | bytes 847880 | tf_op jit(solution)/shard_map/ppermute | solution.py:317
  20.3 0.7 %copy-start.4 = (s32[4]{0:T(128)S(1)}, s32[4]{0:T(128)}, u32[]{:S(2)}) copy-start(s32[4]{0:T(128)} %turn_ref.1) | copy-start | bytes 52
  33.7 4.1 %collective-permute-start.7 = (f32[2,5,8,128]{3,2,1,0:T(8,128)S(1)}, f32[2,5,8,128]{3,2,1,0:T(8,128)S(1)}, u32[]{:S(2)}, u32[]{:S(2)}) collective-permute-start(f32[2,5,8,128]{3,2,1,0:T(8,128)S(1)} %get-tuple-element.26), channel_id=1, source_target_pairs={{0,8},{8,0},{16,24},{24,16},{1,9},{9,1},{17,25},{25,17},{2,10},{10... | collective-permute-start | bytes 122888 | tf_op jit(solution)/shard_map/ppermute | solution.py:308
  34.3 4.0 %collective-permute-start.8 = (f32[2,5,8,128]{3,2,1,0:T(8,128)S(1)}, f32[2,5,8,128]{3,2,1,0:T(8,128)S(1)}, u32[]{:S(2)}, u32[]{:S(2)}) collective-permute-start(f32[2,5,8,128]{3,2,1,0:T(8,128)S(1)} %get-tuple-element.27), channel_id=1, source_target_pairs={{0,16},{8,24},{16,0},{24,8},{1,17},{9,25},{17,1},{25,9},{2,18},{10... | collective-permute-start | bytes 122888 | tf_op jit(solution)/shard_map/ppermute | solution.py:308
  35.5 4.9 %collective-permute-start.9 = (f32[2,5,8,128]{3,2,1,0:T(8,128)S(1)}, f32[2,5,8,128]{3,2,1,0:T(8,128)S(1)}, u32[]{:S(2)}, u32[]{:S(2)}) collective-permute-start(f32[2,5,8,128]{3,2,1,0:T(8,128)S(1)} %get-tuple-element.28), channel_id=1, source_target_pairs={{0,24},{8,16},{16,8},{24,0},{1,25},{9,17},{17,9},{25,1},{2,26},{10... | collective-permute-start | bytes 122888 | tf_op jit(solution)/shard_map/ppermute | solution.py:308
